TPU v7x, 32 devices: a whole 2x2x4 slice. The times are simulated.
32 devices in a mesh: rad: 4 (over x, core), lat: 8 (over z, y).
Axes of the slice: x: 2, y: 2, z: 4, core: 2. Of those that a mesh axis runs over, the one named last changes fastest.
Arguments:
- velocity: bfloat16 [3, 128, 768, 1536], P(None, 'rad', 'lat'), may hold values from -6 to 6
- density: float32 [128], P('rad'), may hold values from 0.3 to 3
- offsets: int32 [4], replicated, may hold values from -3 to 3, as said below
- radial_weights: float32 [2, 4, 128], P(None, None, 'rad'), may hold values from -3 to 3
- angular_scale: float32 [128], P('rad'), may hold values from 9.536743e-07 to 3.8146973e-06
- order_table: int32 [512], replicated, may hold values from 0 to 511, as said below
- eigenfunctions: float32 [512, 32, 128], P(None, None, 'rad'), may hold values from -0.5 to 0.5
Outputs:
- coeffs: float32 [512, 2, 32, 512], P('lat', None, 'rad')
Inputs may be any that keep to these rules, and one draw needn't show every extreme that they name: 4 distinct offsets; minus 3 and 3 are among them. `order_table`: a permutation of the orders; for every k, slots 2k and 2k + 1 hold orders m and 511 - m.
All inputs are finite; a program needn't handle non-finite values.
Results may differ from a plain program's by a relative error of at most 0.0003.
Values sent between devices are 32-bit elements; how exact they have to be, the bound alone decides.
A program may use at most 256 MiB of HBM per device.

v0:
```python
import jax
import jax.numpy as jnp
from jax import lax
from jax.sharding import PartitionSpec as P

TAPS = 4
HALO = 3


def extended(value, sides, width):
    for axis, dim in sides:
        size, length = (lax.axis_size(axis), value.shape[dim])
        up = [(i, (i + 1) % size) for i in range(size - 1)]
        down = [(j, i) for i, j in up]
        last = lax.slice_in_dim(value, length - width, length, axis=dim)
        initial = lax.slice_in_dim(value, 0, width, axis=dim)
        before = lax.ppermute(last, axis, up)
        after = lax.ppermute(initial, axis, down)
        value = jnp.concatenate([before, value, after], axis=dim)
    return value


def legendre_rows(orders, lat_count, degrees):
    colatitude = jnp.pi * (jnp.arange(lat_count, dtype=jnp.float32) + 0.5) / lat_count
    cosine = jnp.cos(colatitude)
    sine = jnp.sin(colatitude)
    order_float = orders.astype(jnp.float32)
    ladder = jnp.arange(1, degrees, dtype=jnp.float32)
    log_steps = jnp.concatenate(
        [
            jnp.zeros((1,), jnp.float32),
            jnp.cumsum(0.5 * jnp.log((2.0 * ladder + 1.0) / (2.0 * ladder))),
        ]
    )
    log_start = 0.5 * jnp.log(jnp.ones((), jnp.float32) * 0.5) + jnp.take(log_steps, orders)
    log_diagonal = log_start[:, None] + order_float[:, None] * jnp.log(sine)[None, :]

    def advance(state, degree):
        previous, older, exponent = state
        level = degree.astype(jnp.float32)
        upward = jnp.sqrt(
            (4.0 * level * level - 1.0)
            / jnp.maximum(level * level - order_float * order_float, 1.0)
        )
        backward = jnp.sqrt(
            jnp.maximum((level - 1.0) * (level - 1.0) - order_float * order_float, 0.0)
            / jnp.maximum(4.0 * (level - 1.0) * (level - 1.0) - 1.0, 1.0)
        )
        recurred = upward[:, None] * (cosine[None, :] * previous - backward[:, None] * older)
        starting = (degree == orders)[:, None]
        scaled = jnp.where(
            starting,
            jnp.ones_like(recurred),
            jnp.where((degree > orders)[:, None], recurred, jnp.zeros_like(recurred)),
        )
        exponent = jnp.where(starting, log_diagonal, exponent)
        ratio = jnp.maximum(jnp.abs(scaled), 1.0)
        scaled = scaled / ratio
        previous = previous / ratio
        exponent = exponent + jnp.log(ratio)
        return ((scaled, previous, exponent), (scaled, exponent))

    zeros = jnp.zeros((orders.shape[0], lat_count), jnp.float32)
    _, outputs = lax.scan(
        advance, (zeros, zeros, zeros), jnp.arange(degrees, dtype=jnp.int32), unroll=32
    )
    rows = outputs[0] * jnp.exp(outputs[1])
    weight = jnp.sqrt(jnp.pi / lat_count) * sine
    return rows * weight[None, None, :]


def spectral_source(part, rows):
    transformed = jnp.einsum("fijco,loj->fiocl", part, rows, precision=lax.Precision.HIGHEST)
    level = jnp.arange(rows.shape[0], dtype=jnp.float32)
    degree_factor = level * (level + 1.0)
    return transformed[0] - degree_factor * transformed[1]


def fourier_table(lon_count, degrees):
    longitude = jnp.arange(lon_count, dtype=jnp.int32)[:, None]
    wave = jnp.arange(degrees, dtype=jnp.int32)[None, :]
    angle = 2.0 * jnp.pi * (longitude * wave % lon_count).astype(jnp.float32) / lon_count
    scale = 1.0 / jnp.sqrt(jnp.ones((), jnp.float32) * lon_count)
    return jnp.concatenate([jnp.cos(angle), -jnp.sin(angle)], axis=1) * scale


def body(velocity, density, offsets, radial_weights, angular_scale, order_table, eigenfunctions):
    shells = velocity.shape[1]
    lat_local = velocity.shape[2]
    lon_count = velocity.shape[3]
    degrees = order_table.shape[0]
    lat_groups = lax.axis_size("lat")
    rad_groups = lax.axis_size("rad")
    per_device = degrees // lat_groups
    lat_count = lat_local * lat_groups
    flow = velocity.astype(jnp.float32)
    radial, polar, azimuth = (flow[0], flow[1], flow[2])
    rho = density[:, None, None]
    cross = jnp.stack([rho * radial * polar, rho * radial * azimuth])
    padded = extended(cross, (("rad", 1),), HALO)
    radial_term = jnp.zeros_like(radial)
    for tap in range(TAPS):
        shifted = lax.dynamic_slice_in_dim(padded, HALO + offsets[tap], shells, 1)
        radial_term = (
            radial_term
            + radial_weights[0, tap][:, None, None] * shifted[0]
            + radial_weights[1, tap][:, None, None] * shifted[1]
        )
    angular_term = (
        angular_scale[:, None, None]
        * rho
        * (polar * polar + azimuth * azimuth - 2.0 * radial * radial + polar * azimuth)
    )
    fields = jnp.stack([radial_term, angular_term]).reshape(2 * shells * lat_local, lon_count)
    spectrum = jnp.dot(
        fields,
        fourier_table(lon_count, degrees),
        precision=lax.Precision.HIGHEST,
        preferred_element_type=jnp.float32,
    ).reshape(2, shells, lat_local, 2, degrees)
    quarter = per_device // rad_groups
    slot_order = (
        order_table.reshape(lat_groups, rad_groups, quarter).transpose(1, 0, 2).reshape(degrees)
    )
    by_slot = jnp.take(spectrum, slot_order, axis=4)
    gathered = lax.all_to_all(
        lax.all_to_all(by_slot, "rad", split_axis=4, concat_axis=1, tiled=True),
        "lat",
        split_axis=4,
        concat_axis=2,
        tiled=True,
    )
    first_slot = lax.axis_index("lat") * per_device + lax.axis_index("rad") * quarter
    my_orders = lax.dynamic_slice_in_dim(order_table, first_slot, quarter)
    rows = legendre_rows(my_orders, lat_count, degrees)
    source = spectral_source(gathered, rows)
    totals = jnp.einsum(
        "rocl,lnr->ocnl",
        source,
        lax.all_gather(eigenfunctions, "rad", axis=2, tiled=True),
        precision=lax.Precision.HIGHEST,
    )
    return lax.all_to_all(totals, "rad", split_axis=2, concat_axis=0, tiled=True)


def solution(mesh):
    placed = (
        P(None, "rad", "lat", None),
        P("rad"),
        P(),
        P(None, None, "rad"),
        P("rad"),
        P(),
        P(None, None, "rad"),
    )
    return jax.shard_map(
        body, mesh=mesh, in_specs=placed, out_specs=P("lat", None, "rad", None), check_vma=False
    )
```

profile of v0, /device:TPU:0, one launch (start us, length us, event | category | flops | bytes accessed | tf_op | source)
XLA Modules:
  0.0 1935.6 jit_solution(9630561268978998743)
XLA Ops:
  6.5 30.5 %convert_element_type.236 = f32[3,32,96,1536]{3,2,1,0:T(8,128)} convert(bf16[3,32,96,1536]{3,2,1,0:T(8,128)(2,1)} %param.9) | non-fusion elementwise | flops 14155776 | bytes 84934656 | tf_op jit(solution)/shard_map/convert_element_type | solution.py:96
  37.1 31.0 %slice_multiply_fusion.1 = (f32[1,32,96,1536]{3,2,1,0:T(8,128)S(1)}, f32[1,32,96,1536]{3,2,1,0:T(8,128)}, f32[1,32,96,1536]{3,2,1,0:T(8,128)}) fusion(f32[3,32,96,1536]{3,2,1,0:T(8,128)} %convert_element_type.236, f32[32]{0:T(128)S(1)} %copy-done.10, f32[32]{0:T(128)S(1)} %mul.3368), kind=kLoop, calls=%fused_computation.397 | loop fusion | flops 56623104 | bytes 113246464 | tf_op jit(solution)/shard_map/mul | solution.py:99
  95.4 13.3 sine_negate_fusion
  112.0 29.2 %pad_maximum_fusion = f32[2,38,96,1536]{3,2,1,0:T(8,128)} fusion(f32[2,3,96,1536]{3,2,1,0:T(8,128)S(1)} %collective-permute-done.1, f32[1,32,96,1536]{3,2,1,0:T(8,128)} %get-tuple-element.831, f32[1,32,96,1536]{3,2,1,0:T(8,128)} %copy-done, f32[2,3,96,1536]{3,2,1,0:T(8,128)} %collective-permute-done), kind=kLoop, calls=%fused_computation.366 | loop fusion | flops 33619968 | bytes 89653248 | tf_op jit(solution)/shard_map/concatenate | solution.py:19
  141.2 55.3 %fusion.112 = f32[1,32,96,1536]{3,2,1,0:T(8,128)} fusion(f32[2,38,96,1536]{3,2,1,0:T(8,128)} %pad_maximum_fusion, s32[]{:T(128)S(6)} %add.1079, s32[]{:T(128)S(6)} %select_n.735, s32[]{:T(128)S(6)} %select_n.734, s32[]{:T(128)S(6)} %select_n.733, s32[]{:T(128)S(6)} %select_n.732, f32[32]{0:T(128)} %get-tuple-element.841, f32[32]{0:T(128)} %get-tuple-element.842, ...), kind=kLoop, calls=%fused_computation.382 | loop fusion | flops 70778880 | bytes 169870352 | tf_op jit(solution)/shard_map/add | solution.py:105
  196.5 128.1 %fusion.103 = f32[2,32,96,2,512]{4,2,3,1,0:T(8,128)} fusion(f32[2,512,1536,1,1]{2,1,0,4,3:T(8,128)} %bitcast.541, f32[1,32,96,1536]{3,2,1,0:T(8,128)} %get-tuple-element.832, f32[1,32,96,1536]{3,2,1,0:T(8,128)} %fusion.112), kind=kOutput, calls=%fused_computation.368 | convolution fusion | flops 115973554176 | bytes 69206016 | tf_op jit(solution)/shard_map/dot_general | solution.py:115
  324.7 36.2 %copy.55 = f32[2,32,96,2,512]{2,1,3,0,4:T(8,128)} copy(f32[2,32,96,2,512]{4,2,3,1,0:T(8,128)} %fusion.103) | data formatting | bytes 50331648 | tf_op jit(solution)/shard_map/dot_general | solution.py:115
  360.8 24.5 %gather_fusion.1 = f32[512,2,32,96,2]{3,2,4,1,0:T(8,128)} fusion(f32[2,32,96,2,512]{2,1,3,0,4:T(8,128)} %copy.55, s32[1024]{0:T(1024)S(1)} %pad_clamp_fusion), kind=kCustom, calls=%fused_computation.1 | custom fusion | bytes 50333696 | tf_op jit(solution)/shard_map/jit(_take)/gather | solution.py:125
  385.4 23.0 %select_bitcast_fusion = f32[2,32,96,2,512]{2,1,3,0,4:T(8,128)} fusion(f32[512,2,32,96,2]{3,2,4,1,0:T(8,128)} %gather_fusion.1, pred[512]{0:T(512)(128)(4,1)S(1)} %compare_and_fusion), kind=kLoop, calls=%fused_computation.371 | loop fusion | flops 6291456 | bytes 50332160 | tf_op jit(solution)/shard_map/jit(_take)/select_n | solution.py:125
  408.4 15.8 all-to-all-start
  429.0 403.0 %all-to-all-done = f32[2,32,96,2,512]{2,1,3,0,4:T(8,128)} async-done(((f32[2,32,96,2,512]{2,1,3,0,4:T(8,128)}), f32[2,32,96,2,512]{2,1,3,0,4:T(8,128)}, u32[]{:S(2)}, u32[]{:S(2)}) %all-to-all-start) | async-done | bytes 25165856 | tf_op jit(solution)/shard_map/all_to_all | solution.py:127
  832.0 36.5 %copy.56 = f32[2,32,96,2,4,128]{5,2,3,1,4,0:T(8,128)} copy(f32[2,32,96,2,4,128]{2,1,3,0,5,4:T(8,128)} %bitcast.31) | data formatting | bytes 50331648 | tf_op jit(solution)/shard_map/all_to_all | solution.py:127
  868.5 25.0 %copy.57 = f32[2,128,96,2,128]{1,2,3,0,4:T(8,128)} copy(f32[2,128,96,2,128]{4,2,3,1,0:T(8,128)} %bitcast.535) | data formatting | bytes 50331648 | tf_op jit(solution)/shard_map/all_to_all | solution.py:127
  899.9 787.2 %while.23 = (s32[]{:T(128)}, f32[16,768]{1,0:T(8,128)S(1)}, f32[16,768]{1,0:T(8,128)S(1)}, f32[16,768]{1,0:T(8,128)S(1)}, f32[16,32,16,768]{3,2,1,0:T(8,128)}, /...) while((s32[]{:T(128)}, f32[16,768]{1,0:T(8,128)S(1)}, ...), condition=%wide.region_3.4_spmd.clone.clone, body=%wide.region_2.3_spmd.clone.clone.sunk | while | flops 8324961 | bytes 17205440 | solution.py:64
  900.7 12.0 broadcast_compare_fusion.66
  935.5 8.6 broadcast_compare_fusion.67
  949.9 12.0 broadcast_compare_fusion.66
  984.6 8.6 broadcast_compare_fusion.67
  999.0 12.0 broadcast_compare_fusion.66
  1033.8 8.6 broadcast_compare_fusion.67
  1048.2 12.0 broadcast_compare_fusion.66
  1083.0 8.6 broadcast_compare_fusion.67
  1097.4 12.0 broadcast_compare_fusion.66
  1146.6 12.0 broadcast_compare_fusion.66
  1181.4 8.6 broadcast_compare_fusion.67
  1195.9 12.0 broadcast_compare_fusion.66
  1230.6 8.6 broadcast_compare_fusion.67
  1245.0 12.0 broadcast_compare_fusion.66
  1294.2 12.0 broadcast_compare_fusion.66
  1329.0 8.6 broadcast_compare_fusion.67
  1343.5 12.0 broadcast_compare_fusion.66
  1378.3 8.6 broadcast_compare_fusion.67
  1392.7 12.0 broadcast_compare_fusion.66
  1427.5 8.6 broadcast_compare_fusion.67
  1442.0 12.0 broadcast_compare_fusion.66
  1491.1 12.0 broadcast_compare_fusion.66
  1525.9 8.6 broadcast_compare_fusion.67
  1540.3 12.0 broadcast_compare_fusion.66
  1589.5 12.0 broadcast_compare_fusion.66
  1624.2 8.6 broadcast_compare_fusion.67
  1638.7 12.0 broadcast_compare_fusion.66
  1673.5 8.6 broadcast_compare_fusion.67
  1687.1 25.6 %exponential_multiply_fusion = f32[16,32,16,768]{3,2,1,0:T(8,128)} fusion(f32[16,32,16,768]{3,2,1,0:T(8,128)} %get-tuple-element.427, f32[16,32,16,768]{3,2,1,0:T(8,128)} %get-tuple-element.428), kind=kLoop, calls=%fused_computation.377 | loop fusion | flops 6291456 | bytes 75497472 | tf_op jit(solution)/shard_map/mul | solution.py:67
  1712.7 11.0 copy.71
  1723.7 26.6 %copy.59 = f32[2,128,8,96,2,16]{1,5,4,3,2,0:T(8,128)} copy(f32[2,128,8,96,2,16]{1,3,4,0,5,2:T(8,128)} %bitcast.36) | data formatting | bytes 50331648 | tf_op jit(solution)/shard_map/all_to_all | solution.py:126
  1750.3 112.4 %fusion.120 = f32[2,128,16,2,512]{1,4,3,0,2:T(8,128)} fusion(f32[2,128,768,2,16]{1,4,3,2,0:T(8,128)} %bitcast.534, f32[512,16,768]{2,1,0:T(8,128)} %bitcast.536, f32[768]{0:T(1024)S(1)} %fusion.138), kind=kOutput, calls=%fused_computation.400 | convolution fusion | flops 38660997120 | bytes 67111936 | tf_op jit(solution)/shard_map/fijco,loj->fiocl/dot_general | solution.py:73
  1869.4 22.6 %fusion.129 = f32[16,2,32,512]{2,0,1,3:T(8,128)} fusion(f32[512,32,128,1]{2,1,3,0:T(8,128)S(1)} %bitcast.538, f32[128,16,2,512]{0,3,2,1:T(8,128)S(1)} %fusion.126), kind=kOutput, calls=%fused_computation.411 | convolution fusion | flops 805306368 | bytes 18874368 | tf_op jit(solution)/shard_map/rocl,lnr->ocnl/dot_general | solution.py:137
  1897.8 28.2 %all_to_all.54 = f32[16,2,32,512]{3,0,1,2:T(8,128)S(1)} all-to-all(f32[16,2,32,512]{3,0,1,2:T(8,128)S(1)} %copy.65), channel_id=1, replica_groups=mesh['rad'=4,'lat'=8] {'rad'}, dimensions={2} | all-to-all | bytes 4194304 | tf_op jit(solution)/shard_map/all_to_all | solution.py:143
  (1028 shorter events, 214.5 us)
Async XLA Ops:
  6.5 30.6 %copy-start.10 = (f32[32]{0:T(128)S(1)}, f32[32]{0:T(128)}, u32[]{:S(2)}) copy-start(f32[32]{0:T(128)} %param.10) | copy-start | bytes 388
  6.5 30.6 %copy-start.11 = (f32[32]{0:T(128)S(1)}, f32[32]{0:T(128)}, u32[]{:S(2)}) copy-start(f32[32]{0:T(128)} %param.13) | copy-start | bytes 388
  68.1 9.7 copy-start
  68.1 16.1 copy-start.8
  68.1 21.8 %copy-start.9 = (s32[512]{0:T(512)S(1)}, s32[512]{0:T(512)}, u32[]{:S(2)}) copy-start(s32[512]{0:T(512)} %param.14) | copy-start | bytes 6148
  77.7 34.3 %collective-permute-start.1 = (f32[2,3,96,1536]{3,2,1,0:T(8,128)}, f32[2,3,96,1536]{3,2,1,0:T(8,128)S(1)}, u32[]{:S(2)}, u32[]{:S(2)}) collective-permute-start(f32[2,3,96,1536]{3,2,1,0:T(8,128)} %get-tuple-element.834), channel_id=1, source_target_pairs={{8,0},{16,8},{24,16},{9,1},{17,9},{25,17},{10,2},{18,10},{26,18},{... | collective-permute-start | bytes 10616840 | tf_op jit(solution)/shard_map/ppermute | solution.py:18
  79.0 33.0 %collective-permute-start = (f32[2,3,96,1536]{3,2,1,0:T(8,128)}, f32[2,3,96,1536]{3,2,1,0:T(8,128)}, u32[]{:S(2)}, u32[]{:S(2)}) collective-permute-start(f32[2,3,96,1536]{3,2,1,0:T(8,128)} %get-tuple-element.833), channel_id=1, source_target_pairs={{0,8},{8,16},{16,24},{1,9},{9,17},{17,25},{2,10},{10,18},{18,26},{... | collective-permute-start | bytes 10616840 | tf_op jit(solution)/shard_map/ppermute | solution.py:17
  408.4 15.8 copy-start.1
  408.4 423.6 %all-to-all-start = ((f32[2,32,96,2,512]{2,1,3,0,4:T(8,128)}), f32[2,32,96,2,512]{2,1,3,0,4:T(8,128)}, u32[]{:S(2)}, u32[]{:S(2)}) async-start(f32[2,32,96,2,512]{2,1,3,0,4:T(8,128)} %select_bitcast_fusion), calls=%async_computation | async-start | bytes 67108864 | tf_op jit(solution)/shard_map/all_to_all | solution.py:127
  424.2 1288.6 %all-gather.2.cloned.1.call-start = ((), (), s32[]{:S(2)}) async-start(), calls=%async_computation.3 | async-start | bytes 10485760 | tf_op jit(solution)/shard_map/all_gather | solution.py:140
  893.5 830.2 %all-to-all-start.1 = ((f32[2,128,96,2,128]{1,2,3,0,4:T(8,128)}), f32[2,128,96,2,128]{1,2,3,0,4:T(8,128)}, u32[]{:S(2)}, u32[]{:S(2)}) async-start(f32[2,128,96,2,128]{1,2,3,0,4:T(8,128)} %copy.57), calls=%async_computation.1 | async-start | bytes 50331648 | tf_op jit(solution)/shard_map/all_to_all | solution.py:126
  944.2 2.4 copy-start.4
  944.3 2.4 copy-start.3
  993.4 2.4 copy-start.4
  993.5 2.4 copy-start.3
  1042.5 2.4 copy-start.4
  1042.6 2.4 copy-start.3
  1091.7 2.4 copy-start.4
  1091.8 2.4 copy-start.3
  1140.9 2.4 copy-start.4
  1141.0 2.4 copy-start.3
  1190.1 2.4 copy-start.4
  1190.2 2.4 copy-start.3
  1193.2 1.9 copy-start.7
  1239.4 2.4 copy-start.4
  1239.5 2.4 copy-start.3
  1288.6 2.4 copy-start.4
  1288.7 2.4 copy-start.3
  1337.7 2.4 copy-start.4
  1337.9 2.4 copy-start.3
  1340.8 2.0 copy-start.7
  1387.0 2.4 copy-start.4
  1387.2 2.4 copy-start.3
  1436.2 2.4 copy-start.4
  1436.3 2.4 copy-start.3
  1439.2 2.0 copy-start.7
  1485.5 2.4 copy-start.4
  1485.6 2.4 copy-start.3
  1534.6 2.4 copy-start.4
  1534.8 2.4 copy-start.3
  1583.8 2.4 copy-start.4
  1583.9 2.4 copy-start.3
  1633.0 2.4 copy-start.4
  1633.1 2.4 copy-start.3
  1682.2 2.4 copy-start.4
  1682.3 2.4 copy-start.3
  1723.7 145.6 %slice-start = ((s8[8388608]{0:T(1024)(128)(4,1)}), s8[4194304]{0:T(1024)(128)(4,1)S(1)}, s32[]{:S(2)}) async-start(s8[8388608]{0:T(1024)(128)(4,1)} %bitcast.537), calls=%async_computation.4 | async-start | bytes 8388608
  1750.3 119.1 %slice-start.1 = ((s8[8388608]{0:T(1024)(128)(4,1)}), s8[4194304]{0:T(1024)(128)(4,1)S(1)}, s32[]{:S(2)}) async-start(s8[8388608]{0:T(1024)(128)(4,1)} %bitcast.537), calls=%async_computation.5 | async-start | bytes 8388608
  (61 other events, 79.6 us)
Sparse Core Ops, SparseCore 0:
  426.9 111.5 all-gather.1
where the time goes:
time: 1950 us; the launch traced here: 1940 us
  other arithmetic  633 us (32%)
  waiting for transfers between devices  403 us (21%)
  loops' own time  330 us (17%)
  matrix products  263 us (13%)
  local copies, waits for them, and re-layouts  231 us (12%)
  starting transfers between devices  28.5 us (1%)
  blocking collectives  28.2 us (1%)
    all_to_all x1, waiting for transfers between devices, body(): lax.all_to_all(by_slot, 'rad', split_axis=4, concat_axis=1, tiled=True)  403 us
    another operation x1, loops' own time, legendre_rows(): lax.scan(advance, (zeros, zeros, zeros), jnp.arange(degrees, dtype=jnp.in...  330 us
    gt x32, other arithmetic, advance(): degree > orders  330 us
    dot_general x1, matrix products, body(): jnp.dot(fields, fourier_table(lon_count, degrees), precision=lax.Precisio...  128 us
    dot_general x1, matrix products, spectral_source(): jnp.einsum('fijco,loj->fiocl', part, rows, precision=lax.Precision.HIGHEST)  112 us
    all_to_all x2, local copies, waits for them, and re-layouts, body(): lax.all_to_all(by_slot, 'rad', split_axis=4, concat_axis=1, tiled=True)  61.5 us
    add x1, other arithmetic, body(): radial_term + radial_weights[0, tap][:, None, None] * shifted[0]  55.3 us
    while x512, other arithmetic  50.5 us
  transfers between devices with their start and end apart: 5, of which 1 were waited for; matrix products, arithmetic and copies ran while one was open for 30% of the time, Pallas kernels for 0%

commit v1 on v0

v1 whole, which is shorter than its diff:
```python
import math

import jax
import jax.numpy as jnp
from jax import lax
from jax.experimental import pallas as pl
from jax.experimental.pallas import tpu as pltpu
from jax.sharding import PartitionSpec as P

TAPS = 4
HALO = 3
STEP = 8
LANES = 128
SHIFT = 60
CHUNKS = 4
HIGH = lax.Precision.HIGH


def extended(value, sides, width):
    for axis, dim in sides:
        size, length = (lax.axis_size(axis), value.shape[dim])
        up = [(i, (i + 1) % size) for i in range(size - 1)]
        down = [(j, i) for i, j in up]
        last = lax.slice_in_dim(value, length - width, length, axis=dim)
        initial = lax.slice_in_dim(value, 0, width, axis=dim)
        before = lax.ppermute(last, axis, up)
        after = lax.ppermute(initial, axis, down)
        value = jnp.concatenate([before, value, after], axis=dim)
    return value


def ladder_kernel(up_ref, down_ref, cosine_ref, first_ref, power_ref, order_ref, weight_ref, out_ref,
                  now, older, power):
    block = pl.program_id(0)

    @pl.when(block == 0)
    def _():
        now[...] = jnp.zeros_like(now)
        older[...] = jnp.zeros_like(older)
        power[...] = power_ref[...]

    current, previous, scale = now[...], older[...], power[...]
    factor = jnp.where(
        scale == 0.0,
        1.0,
        jnp.where(
            scale == -1.0, 2.0**-SHIFT, jnp.where(scale == -2.0, 2.0 ** (-2 * SHIFT), 0.0)
        ),
    )
    factor = factor * weight_ref[...]
    cosine = cosine_ref[...]
    first = first_ref[...]
    orders = order_ref[...]
    for i in range(STEP):
        recurred = up_ref[0, :, i : i + 1] * (cosine * current) - down_ref[0, :, i : i + 1] * previous
        begins = orders == block * STEP + i
        recurred = recurred + jnp.where(begins, first, 0.0)
        previous = current
        current = recurred
        out_ref[i] = recurred * factor
    large = jnp.maximum(jnp.abs(current), jnp.abs(previous)) > 2.0**SHIFT
    shrink = jnp.where(large, 2.0**-SHIFT, 1.0)
    now[...] = current * shrink
    older[...] = previous * shrink
    power[...] = scale + jnp.where(large, 1.0, 0.0)


def legendre_rows(orders, first_lat, lat_local, lat_count, degrees):
    count = orders.shape[0]
    padded = -(-lat_local // LANES) * LANES
    lat = first_lat + jnp.minimum(jnp.arange(padded, dtype=jnp.int32), lat_local - 1)
    colatitude = jnp.pi * (lat.astype(jnp.float32) + 0.5) / lat_count
    cosine = jnp.cos(colatitude)
    sine = jnp.sin(colatitude)
    order_float = orders.astype(jnp.float32)
    ladder = jnp.arange(1, degrees, dtype=jnp.float32)
    log_steps = jnp.concatenate(
        [
            jnp.zeros((1,), jnp.float32),
            jnp.cumsum(0.5 * jnp.log((2.0 * ladder + 1.0) / (2.0 * ladder))),
        ]
    )
    log_start = 0.5 * jnp.log(jnp.ones((), jnp.float32) * 0.5) + jnp.take(log_steps, orders)
    log_diagonal = log_start[:, None] + order_float[:, None] * jnp.log(sine)[None, :]
    unit = SHIFT * 0.6931471805599453
    power = jnp.minimum(jnp.floor(log_diagonal / unit), 0.0)
    coarse = 41.5
    first = jnp.exp((log_diagonal - power * coarse) - power * (unit - coarse))
    level = jnp.arange(degrees, dtype=jnp.float32)[None, :]
    square = (order_float * order_float)[:, None]
    upward = jnp.sqrt((4.0 * level * level - 1.0).clip(0.0) / jnp.maximum(level * level - square, 1.0))
    below = (level - 1.0) * (level - 1.0)
    backward = jnp.sqrt(
        jnp.maximum(below - square, 0.0) / jnp.maximum(4.0 * below - 1.0, 1.0)
    )

    def stepped(value):
        return value.reshape(count, degrees // STEP, STEP).transpose(1, 0, 2)

    weight = jnp.where(
        jnp.arange(padded) < lat_local, jnp.sqrt(jnp.pi / lat_count) * sine, 0.0
    )
    whole = pl.BlockSpec((count, padded), lambda k: (0, 0))
    row = pl.BlockSpec((1, padded), lambda k: (0, 0))
    coefficient = pl.BlockSpec((1, count, STEP), lambda k: (k, 0, 0))
    return pl.pallas_call(
        ladder_kernel,
        grid=(degrees // STEP,),
        in_specs=[coefficient, coefficient, row, whole, whole, whole, row],
        out_specs=pl.BlockSpec((STEP, count, padded), lambda k: (k, 0, 0)),
        out_shape=jax.ShapeDtypeStruct((degrees, count, padded), jnp.float32),
        scratch_shapes=[pltpu.VMEM((count, padded), jnp.float32)] * 3,
        compiler_params=pltpu.CompilerParams(vmem_limit_bytes=16 << 20),
        cost_estimate=pl.CostEstimate(
            flops=20 * degrees * count * padded,
            bytes_accessed=4 * degrees * count * padded,
            transcendentals=0,
        ),
    )(
        stepped(upward),
        stepped(upward * backward),
        cosine[None, :],
        first,
        power,
        jnp.broadcast_to(orders[:, None], (count, padded)),
        weight[None, :],
    )


def split(value):
    high = value.astype(jnp.bfloat16)
    return high, (value - high.astype(jnp.float32)).astype(jnp.bfloat16)


def degree_kernel(rows_ref, part_ref, out_ref):
    degrees = rows_ref.shape[0]
    half = part_ref.shape[1] // 2
    shells = out_ref.shape[3]
    level = lax.broadcasted_iota(jnp.int32, (degrees, half), 0).astype(jnp.float32)
    factor = level * (level + 1.0)
    contract = (((1,), (1,)), ((), ()))
    for o in range(part_ref.shape[0]):
        rows_high, rows_low = split(rows_ref[:, o, :])
        high, low = split(part_ref[o])
        both = jnp.concatenate([rows_high, rows_low], axis=1)
        twice = jnp.concatenate([high, high], axis=1)
        sums = lax.dot_general(both, twice, contract, preferred_element_type=jnp.float32)
        sums = sums + lax.dot_general(rows_high, low, contract, preferred_element_type=jnp.float32)
        source = sums[:, :half] - factor * sums[:, half:]
        for c in range(2):
            out_ref[c, :, o, :] = source[:, c * shells : (c + 1) * shells]


def spectral_source(part, rows, first, count):
    degrees, _, padded = rows.shape
    columns = part.shape[1]
    shells = columns // 4
    group = 8
    skip = first // group
    return pl.pallas_call(
        degree_kernel,
        grid=(count // group,),
        in_specs=[
            pl.BlockSpec((degrees, group, padded), lambda k: (0, skip + k, 0)),
            pl.BlockSpec((group, columns, padded), lambda k: (k, 0, 0)),
        ],
        out_specs=pl.BlockSpec((2, degrees, group, shells), lambda k: (0, 0, k, 0)),
        out_shape=jax.ShapeDtypeStruct((2, degrees, count, shells), jnp.float32),
        compiler_params=pltpu.CompilerParams(vmem_limit_bytes=48 << 20),
        cost_estimate=pl.CostEstimate(
            flops=6 * degrees * count * columns * padded,
            bytes_accessed=4 * count * (degrees * padded + columns * padded + degrees * 2 * shells),
            transcendentals=0,
        ),
    )(rows, part)


def fourier_table(lon_count, orders):
    longitude = jnp.arange(lon_count, dtype=jnp.int32)[None, :, None]
    angle = (
        2.0
        * jnp.pi
        * (longitude * orders[:, None, :] % lon_count).astype(jnp.float32)
        / lon_count
    )
    scale = 1.0 / jnp.sqrt(jnp.ones((), jnp.float32) * lon_count)
    return jnp.concatenate([jnp.cos(angle), -jnp.sin(angle)], axis=2) * scale


def body(velocity, density, offsets, radial_weights, angular_scale, order_table, eigenfunctions):
    shells = velocity.shape[1]
    lat_local = velocity.shape[2]
    lon_count = velocity.shape[3]
    degrees = order_table.shape[0]
    lat_groups = lax.axis_size("lat")
    rad_groups = lax.axis_size("rad")
    per_device = degrees // lat_groups
    lat_count = lat_local * lat_groups
    flow = velocity.astype(jnp.float32)
    radial, polar, azimuth = (flow[0], flow[1], flow[2])
    rho = density[:, None, None]
    cross = jnp.stack([rho * radial * polar, rho * radial * azimuth])
    padded = extended(cross, (("rad", 1),), HALO)
    radial_term = jnp.zeros_like(radial)
    for tap in range(TAPS):
        shifted = lax.dynamic_slice_in_dim(padded, HALO + offsets[tap], shells, 1)
        radial_term = (
            radial_term
            + radial_weights[0, tap][:, None, None] * shifted[0]
            + radial_weights[1, tap][:, None, None] * shifted[1]
        )
    angular_term = (
        angular_scale[:, None, None]
        * rho
        * (polar * polar + azimuth * azimuth - 2.0 * radial * radial + polar * azimuth)
    )
    fields = jnp.stack([radial_term, angular_term]).reshape(2 * shells * lat_local, lon_count)
    quarter = per_device // rad_groups
    count = degrees // rad_groups
    chunks = math.gcd(CHUNKS, quarter)
    size = count // chunks
    slot_order = (
        order_table.reshape(lat_groups, rad_groups, chunks, quarter // chunks)
        .transpose(1, 2, 0, 3)
        .reshape(rad_groups, chunks, size)
    )
    received = []
    for chunk in range(chunks):
        spectrum = jnp.einsum(
            "dkx,nk->dxn",
            fourier_table(lon_count, slot_order[:, chunk]),
            fields,
            precision=HIGH,
            preferred_element_type=jnp.float32,
        )
        received.append(
            lax.all_to_all(spectrum, "rad", split_axis=0, concat_axis=0, tiled=True)
        )
    my_orders = lax.dynamic_index_in_dim(
        slot_order, lax.axis_index("rad"), 0, keepdims=False
    ).reshape(count)
    rows = legendre_rows(
        my_orders, lax.axis_index("lat") * lat_local, lat_local, lat_count, degrees
    )
    modes = lax.all_gather(eigenfunctions, "rad", axis=2, tiled=True)
    mine = []
    for chunk in range(chunks):
        part = received[chunk].reshape(rad_groups, 2, size, 2, shells, lat_local)
        part = jnp.pad(part, ((0, 0),) * 5 + ((0, rows.shape[2] - lat_local),))
        part = part.transpose(2, 3, 1, 0, 4, 5).reshape(size, 4 * rad_groups * shells, -1)
        source = spectral_source(part, rows, chunk * size, size)
        totals = jnp.einsum("clor,lnr->ocnl", source, modes, precision=HIGH)
        mine.append(lax.psum_scatter(totals, "lat", scatter_dimension=0, tiled=True))
    mine = jnp.concatenate(mine, axis=0)
    return lax.all_to_all(mine, "rad", split_axis=2, concat_axis=0, tiled=True)


def solution(mesh):
    placed = (
        P(None, "rad", "lat", None),
        P("rad"),
        P(),
        P(None, None, "rad"),
        P("rad"),
        P(),
        P(None, None, "rad"),
    )
    return jax.shard_map(
        body, mesh=mesh, in_specs=placed, out_specs=P("lat", None, "rad", None), check_vma=False
    )
```

time: 1950 us -> 1170 us (0.60)
  other arithmetic: 633 us -> 206 us
  loops' own time: 330 us -> 0 us
  Pallas kernels: 0 us -> 187 us
  waiting for transfers between devices: 403 us -> 247 us
  matrix products: 263 us -> 176 us
  local copies, waits for them, and re-layouts: 231 us -> 144 us
  blocking collectives: 28.2 us -> 103 us
  starting transfers between devices: 28.5 us -> 86.2 us
    another operation x1 -> x0, loops' own time: 330 us -> none  [legendre_rows(): lax.scan(advance, (zeros, zeros, zeros), jnp.arange(degrees, dtype=jnp.in...]
    gt x32 -> x0, other arithmetic: 330 us -> none  [advance(): degree > orders]
    all_to_all x2 -> x3, waiting for transfers between devices: 403 us -> 158 us  [body(): lax.all_to_all(spectrum, 'rad', split_axis=0, concat_axis=0, tiled=True)]
    pallas_call x0 -> x5, Pallas kernels: none -> 187 us  [the longest x4 149 us: spectral_source(): pl.pallas_call(degree_kernel, grid=(count // group,), in_specs=[pl.BlockS...]
    reduce_scatter x0 -> x4, waiting for transfers between devices: none -> 88.4 us  [body(): lax.psum_scatter(totals, 'lat', scatter_dimension=0, tiled=True)]
    all_to_all x4 -> x1, local copies, waits for them, and re-layouts: 90.6 us -> 2.54 us  [body(): return lax.all_to_all(mine, 'rad', split_axis=2, concat_axis=0, tiled=True)]
    dot_general x3 -> x8, matrix products: 263 us -> 176 us  [the longest x4 91 us: body(): totals = jnp.einsum('clor,lnr->ocnl', source, modes, precision=HIGH)]
    all_to_all x1 -> x2, blocking collectives: 28.2 us -> 103 us  [the longest x1 74.4 us: body(): lax.all_to_all(spectrum, 'rad', split_axis=0, concat_axis=0, tiled=True)]
  transfers between devices with their start and end apart: 5 -> 10, of which waited for: 1 -> 4; matrix products, arithmetic and copies ran while one was open for 30% -> 35% of each run, Pallas kernels for 0% -> 16%
where the time goes in v1:
time: 1170 us
  waiting for transfers between devices  247 us (21%)
  other arithmetic  206 us (18%)
  Pallas kernels  187 us (16%)
  matrix products  176 us (15%)
  local copies, waits for them, and re-layouts  144 us (12%)
  blocking collectives  103 us (9%)
  starting transfers between devices  86.2 us (7%)
  between operations  18.8 us (2%)
    all_to_all x3, waiting for transfers between devices, body(): lax.all_to_all(spectrum, 'rad', split_axis=0, concat_axis=0, tiled=True)  158 us
    pallas_call x4, Pallas kernels, spectral_source(): pl.pallas_call(degree_kernel, grid=(count // group,), in_specs=[pl.BlockS...  149 us
    dot_general x4, matrix products, body(): totals = jnp.einsum('clor,lnr->ocnl', source, modes, precision=HIGH)  91 us
    reduce_scatter x4, waiting for transfers between devices, body(): lax.psum_scatter(totals, 'lat', scatter_dimension=0, tiled=True)  88.4 us
    dot_general x4, matrix products, body(): jnp.einsum('dkx,nk->dxn', fourier_table(lon_count, slot_order[:, chunk]),...  85.2 us
    all_to_all x3, starting transfers between devices, body(): lax.all_to_all(spectrum, 'rad', split_axis=0, concat_axis=0, tiled=True)  82.2 us
    all_to_all x1, blocking collectives, body(): lax.all_to_all(spectrum, 'rad', split_axis=0, concat_axis=0, tiled=True)  74.4 us
    add x1, other arithmetic, body(): radial_term + radial_weights[0, tap][:, None, None] * shifted[0]  55.8 us
  transfers between devices with their start and end apart: 10, of which 4 were waited for; matrix products, arithmetic and copies ran while one was open for 35% of the time, Pallas kernels for 16%

profile of v1, /device:TPU:0, one launch (start us, length us, event | category | flops | bytes accessed | tf_op | source)
XLA Modules:
  0.0 1167.2 jit_solution(10880126200844236868)
XLA Ops:
  6.5 30.5 %convert_element_type.53 = f32[3,32,96,1536]{3,2,1,0:T(8,128)} convert(bf16[3,32,96,1536]{3,2,1,0:T(8,128)(2,1)} %param.7) | non-fusion elementwise | flops 14155776 | bytes 84934656 | tf_op jit(solution)/shard_map/convert_element_type | solution.py:199
  37.1 31.0 %slice_multiply_fusion.1 = (f32[1,32,96,1536]{3,2,1,0:T(8,128)S(1)}, f32[1,32,96,1536]{3,2,1,0:T(8,128)}, f32[1,32,96,1536]{3,2,1,0:T(8,128)}) fusion(f32[3,32,96,1536]{3,2,1,0:T(8,128)} %convert_element_type.53, f32[32]{0:T(128)S(1)} %copy-done.9, f32[32]{0:T(128)S(1)} %mul.385), kind=kLoop, calls=%fused_computation.23 | loop fusion | flops 56623104 | bytes 113246464 | tf_op jit(solution)/shard_map/mul | solution.py:202
  68.2 8.5 pad_maximum_fusion.3
  95.3 4.5 fusion.65
  99.8 30.3 %pad_maximum_fusion = f32[2,38,96,1536]{3,2,1,0:T(8,128)} fusion(f32[2,3,96,1536]{3,2,1,0:T(8,128)} %collective-permute-done.1, f32[1,32,96,1536]{3,2,1,0:T(8,128)} %get-tuple-element.6, f32[1,32,96,1536]{3,2,1,0:T(8,128)} %copy-done, f32[2,3,96,1536]{3,2,1,0:T(8,128)S(1)} %collective-permute-done), kind=kLoop, calls=%fused_computation.1 | loop fusion | flops 33619968 | bytes 89653248 | tf_op jit(solution)/shard_map/concatenate | solution.py:28
  130.1 55.8 %fusion.3 = f32[1,32,96,1536]{3,2,1,0:T(8,128)} fusion(f32[2,38,96,1536]{3,2,1,0:T(8,128)} %pad_maximum_fusion, s32[]{:T(128)S(6)} %add.304, s32[]{:T(128)S(6)} %select_n.82, s32[]{:T(128)S(6)} %select_n.81, s32[]{:T(128)S(6)} %select_n.80, s32[]{:T(128)S(6)} %select_n.79, f32[32]{0:T(128)} %get-tuple-element.22, f32[32]{0:T(128)} %get-tuple-element.23, ...), kind=kLoop, calls=%fused_computation.8 | loop fusion | flops 70778880 | bytes 169870352 | tf_op jit(solution)/shard_map/add | solution.py:208
  185.9 29.6 %pad_maximum_fusion.1 = f32[2,32,96,1536]{3,2,1,0:T(8,128)} fusion(f32[1,32,96,1536]{3,2,1,0:T(8,128)} %get-tuple-element.7, f32[1,32,96,1536]{3,2,1,0:T(8,128)} %fusion.3), kind=kLoop, calls=%fused_computation.2 | loop fusion | flops 9437184 | bytes 75497472 | tf_op jit(solution)/shard_map/stack | solution.py:217
  215.6 21.7 %fusion.30 = f32[4,64,6144]{2,1,0:T(8,128)} fusion(f32[6144,1536,1]{1,0,2:T(8,128)} %bitcast.77, f32[4,1536,32]{1,2,0:T(8,128)S(1)} %copy-done.2, f32[4,1536,32]{1,2,0:T(8,128)S(1)} %copy-done.1), kind=kOutput, calls=%fused_computation.43 | convolution fusion | flops 14496301056 | bytes 45613056 | tf_op jit(solution)/shard_map/dkx,nk->dxn/dot_general | solution.py:229
  237.2 71.4 %all-to-all-start = ((f32[4,64,6144]{2,1,0:T(8,128)}), f32[4,64,6144]{2,1,0:T(8,128)}, u32[]{:S(2)}, u32[]{:S(2)}) async-start(f32[4,64,6144]{2,1,0:T(8,128)} %fusion.30), calls=%async_computation | async-start | bytes 12582912 | tf_op jit(solution)/shard_map/all_to_all | solution.py:237
  314.7 38.0 %shard_map.73.rows_ref = f32[512,128,128]{2,1,0:T(8,128)} custom-call(f32[64,128,8]{2,1,0:T(8,128)S(1)} %get-tuple-element.11.up_ref, f32[64,128,8]{2,1,0:T(8,128)S(1)} %get-tuple-element.10.down_ref, f32[1,128]{1,0:T(1,128)S(1)} %get-tuple-element.41.cosine_ref, f32[128,128]{1,0:T(8,128)S(1)} %get-tuple-element.33.first_ref, ...), custom_call_target="tpu_custom_call" | custom-call | flops 167772160 | bytes 33554432 | tf_op jit(solution)/shard_map/pallas_call | solution.py:106
  355.9 23.5 %all-to-all-done = f32[4,64,6144]{2,1,0:T(8,128)} async-done(((f32[4,64,6144]{2,1,0:T(8,128)}), f32[4,64,6144]{2,1,0:T(8,128)}, u32[]{:S(2)}, u32[]{:S(2)}) %all-to-all-start) | async-done | bytes 6291488 | tf_op jit(solution)/shard_map/all_to_all | solution.py:237
  379.4 9.1 reshape.269
  388.5 4.4 copy.69
  392.9 4.3 pad.17
  397.2 37.5 %shard_map.74 = f32[2,512,32,128]{3,2,1,0:T(8,128)} custom-call(f32[512,128,128]{2,1,0:T(8,128)} %shard_map.73.rows_ref, f32[32,512,128]{2,1,0:T(8,128)} %bitcast.82), custom_call_target="tpu_custom_call" | custom-call | flops 6442450944 | bytes 33554432 | tf_op jit(solution)/shard_map/pallas_call | solution.py:160
  434.8 11.0 copy.89
  445.7 22.6 %fusion.18 = f32[32,2,32,512]{2,0,1,3:T(8,128)} fusion(f32[512,32,128,1]{2,1,3,0:T(8,128)} %copy.89, f32[2,512,32,128]{3,2,1,0:T(8,128)} %shard_map.74), kind=kOutput, calls=%fused_computation.33 | convolution fusion | flops 805306368 | bytes 29360128 | tf_op jit(solution)/shard_map/clor,lnr->ocnl/dot_general | solution.py:252
  468.3 11.4 copy.73
  479.8 21.9 %fusion.33 = f32[4,64,6144]{2,1,0:T(8,128)} fusion(f32[6144,1536,1]{1,0,2:T(8,128)} %bitcast.78, f32[4,1536,32]{1,2,0:T(8,128)S(1)} %get-tuple-element.27, f32[4,1536,32]{1,2,0:T(8,128)S(1)} %get-tuple-element.26), kind=kOutput, calls=%fused_computation.47 | convolution fusion | flops 14496301056 | bytes 45613056 | tf_op jit(solution)/shard_map/dkx,nk->dxn/dot_general | solution.py:229
  501.7 5.4 all-to-all-start.1
  507.1 3.2 fusion.55
  510.4 67.4 %all-to-all-done.1 = f32[4,64,6144]{2,1,0:T(8,128)} async-done(((f32[4,64,6144]{2,1,0:T(8,128)}), f32[4,64,6144]{2,1,0:T(8,128)}, u32[]{:S(2)}, u32[]{:S(2)}) %all-to-all-start.1) | async-done | bytes 6291488 | tf_op jit(solution)/shard_map/all_to_all | solution.py:237
  577.7 9.3 reshape.271
  587.0 4.4 copy.74
  591.5 4.3 pad.18
  595.8 37.2 %shard_map.75 = f32[2,512,32,128]{3,2,1,0:T(8,128)} custom-call(f32[512,128,128]{2,1,0:T(8,128)} %shard_map.73.rows_ref, f32[32,512,128]{2,1,0:T(8,128)} %bitcast.83), custom_call_target="tpu_custom_call" | custom-call | flops 6442450944 | bytes 33554432 | tf_op jit(solution)/shard_map/pallas_call | solution.py:160
  632.9 22.9 %fusion.21 = f32[32,2,32,512]{2,0,1,3:T(8,128)} fusion(f32[512,32,128,1]{2,1,3,0:T(8,128)} %copy.89, f32[2,512,32,128]{3,2,1,0:T(8,128)} %shard_map.75), kind=kOutput, calls=%fused_computation.34 | convolution fusion | flops 805306368 | bytes 29360128 | tf_op jit(solution)/shard_map/clor,lnr->ocnl/dot_general | solution.py:252
  655.8 11.4 copy.77
  667.3 21.8 %fusion.36 = f32[4,64,6144]{2,1,0:T(8,128)} fusion(f32[6144,1536,1]{1,0,2:T(8,128)} %bitcast.79, f32[4,1536,32]{1,2,0:T(8,128)S(1)} %get-tuple-element.29, f32[4,1536,32]{1,2,0:T(8,128)S(1)} %get-tuple-element.28), kind=kOutput, calls=%fused_computation.51 | convolution fusion | flops 14496301056 | bytes 45613056 | tf_op jit(solution)/shard_map/dkx,nk->dxn/dot_general | solution.py:229
  689.1 5.4 all-to-all-start.2
  694.5 3.2 fusion.52
  697.8 67.4 %all-to-all-done.2 = f32[4,64,6144]{2,1,0:T(8,128)} async-done(((f32[4,64,6144]{2,1,0:T(8,128)}), f32[4,64,6144]{2,1,0:T(8,128)}, u32[]{:S(2)}, u32[]{:S(2)}) %all-to-all-start.2) | async-done | bytes 6291488 | tf_op jit(solution)/shard_map/all_to_all | solution.py:237
  765.2 9.3 reshape.273
  774.5 4.4 copy.78
  778.9 4.3 pad.19
  783.2 37.2 %shard_map.76 = f32[2,512,32,128]{3,2,1,0:T(8,128)} custom-call(f32[512,128,128]{2,1,0:T(8,128)} %shard_map.73.rows_ref, f32[32,512,128]{2,1,0:T(8,128)} %bitcast.84), custom_call_target="tpu_custom_call" | custom-call | flops 6442450944 | bytes 33554432 | tf_op jit(solution)/shard_map/pallas_call | solution.py:160
  820.3 22.8 %fusion.24 = f32[32,2,32,512]{2,0,1,3:T(8,128)} fusion(f32[512,32,128,1]{2,1,3,0:T(8,128)} %copy.89, f32[2,512,32,128]{3,2,1,0:T(8,128)} %shard_map.76), kind=kOutput, calls=%fused_computation.35 | convolution fusion | flops 805306368 | bytes 29360128 | tf_op jit(solution)/shard_map/clor,lnr->ocnl/dot_general | solution.py:252
  843.2 11.4 copy.81
  854.7 19.8 %fusion.39 = f32[4,64,6144]{2,1,0:T(8,128)S(1)} fusion(f32[6144,1536,1]{1,0,2:T(8,128)} %bitcast.80, f32[4,1536,32]{1,2,0:T(8,128)S(1)} %get-tuple-element.31, f32[4,1536,32]{1,2,0:T(8,128)S(1)} %get-tuple-element.30), kind=kOutput, calls=%fused_computation.55 | convolution fusion | flops 14496301056 | bytes 45613056 | tf_op jit(solution)/shard_map/dkx,nk->dxn/dot_general | solution.py:229
  874.5 74.4 %all_to_all.38 = f32[4,64,6144]{2,1,0:T(8,128)} all-to-all(f32[4,64,6144]{2,1,0:T(8,128)S(1)} %fusion.39), channel_id=1, replica_groups=mesh['rad'=4,'lat'=8] {'rad'}, dimensions={0} | all-to-all | bytes 12582912 | tf_op jit(solution)/shard_map/all_to_all | solution.py:237
  948.9 9.1 reshape.275
  958.0 4.4 copy.82
  962.4 4.4 pad.20
  966.8 37.2 %shard_map.77 = f32[2,512,32,128]{3,2,1,0:T(8,128)} custom-call(f32[512,128,128]{2,1,0:T(8,128)} %shard_map.73.rows_ref, f32[32,512,128]{2,1,0:T(8,128)} %bitcast.81), custom_call_target="tpu_custom_call" | custom-call | flops 6442450944 | bytes 33554432 | tf_op jit(solution)/shard_map/pallas_call | solution.py:160
  1004.0 22.7 %fusion.27 = f32[32,2,32,512]{2,0,1,3:T(8,128)} fusion(f32[512,32,128,1]{2,1,3,0:T(8,128)} %copy.89, f32[2,512,32,128]{3,2,1,0:T(8,128)} %shard_map.77), kind=kOutput, calls=%fused_computation.36 | convolution fusion | flops 805306368 | bytes 29360128 | tf_op jit(solution)/shard_map/clor,lnr->ocnl/dot_general | solution.py:252
  1026.7 11.4 copy.85
  1038.3 88.4 %reduce-scatter.11.cloned.1.call-done = f32[4,2,32,512]{3,2,1,0:T(8,128)} async-done(((f32[32,2,32,512]{3,2,1,0:T(8,128)}), f32[4,2,32,512]{3,2,1,0:T(8,128)}) %reduce-scatter.11.cloned.1.call-update) | async-done | bytes 524304 | tf_op jit(solution)/shard_map/reduce_scatter | solution.py:253
  1129.6 28.2 %all_to_all.39 = f32[16,2,32,512]{3,0,1,2:T(8,128)S(1)} all-to-all(f32[16,2,32,512]{3,0,1,2:T(8,128)S(1)} %copy.86), channel_id=1, replica_groups=mesh['rad'=4,'lat'=8] {'rad'}, dimensions={2} | all-to-all | bytes 4194304 | tf_op jit(solution)/shard_map/all_to_all | solution.py:255
  (80 shorter events, 28.4 us)
Async XLA Ops:
  6.5 30.6 %copy-start.10 = (f32[32]{0:T(128)S(1)}, f32[32]{0:T(128)}, u32[]{:S(2)}) copy-start(f32[32]{0:T(128)} %param.11) | copy-start | bytes 388
  6.5 30.6 %copy-start.9 = (f32[32]{0:T(128)S(1)}, f32[32]{0:T(128)}, u32[]{:S(2)}) copy-start(f32[32]{0:T(128)} %param.8) | copy-start | bytes 388
  6.5 428.2 %all-gather.2.cloned.1.call-start = ((), (), s32[]{:S(2)}) async-start(), calls=%async_computation.9 | async-start | bytes 10485760 | tf_op jit(solution)/shard_map/all_gather | solution.py:245
  68.2 10.5 copy-start
  68.2 14.3 %copy-start.3 = (f32[512,32,32]{0,2,1:T(8,128)S(1)}, f32[512,32,32]{0,2,1:T(8,128)}, u32[]{:S(2)}) copy-start(f32[512,32,32]{0,2,1:T(8,128)} %param.13) | copy-start | bytes 6291460
  68.2 16.9 %copy-start.6 = (s32[4]{0:T(128)S(1)}, s32[4]{0:T(128)}, u32[]{:S(2)}) copy-start(s32[4]{0:T(128)} %param.9) | copy-start | bytes 52
  68.2 22.7 %copy-start.8 = (s32[512]{0:T(512)S(1)}, s32[512]{0:T(512)}, u32[]{:S(2)}) copy-start(s32[512]{0:T(512)} %param.12) | copy-start | bytes 6148
  68.2 25.9 %copy-start.7 = (f32[2,4,32]{2,1,0:T(4,128)S(1)}, f32[2,4,32]{2,1,0:T(4,128)}, u32[]{:S(2)}) copy-start(f32[2,4,32]{2,1,0:T(4,128)} %param.10) | copy-start | bytes 3076
  78.6 21.2 %collective-permute-start = (f32[2,3,96,1536]{3,2,1,0:T(8,128)}, f32[2,3,96,1536]{3,2,1,0:T(8,128)S(1)}, u32[]{:S(2)}, u32[]{:S(2)}) collective-permute-start(f32[2,3,96,1536]{3,2,1,0:T(8,128)} %get-tuple-element.8), channel_id=1, source_target_pairs={{0,8},{8,16},{16,24},{1,9},{9,17},{17,25},{2,10},{10,18},{18,26},{... | collective-permute-start | bytes 10616840 | tf_op jit(solution)/shard_map/ppermute | solution.py:26
  81.2 18.6 %collective-permute-start.1 = (f32[2,3,96,1536]{3,2,1,0:T(8,128)}, f32[2,3,96,1536]{3,2,1,0:T(8,128)}, u32[]{:S(2)}, u32[]{:S(2)}) collective-permute-start(f32[2,3,96,1536]{3,2,1,0:T(8,128)} %get-tuple-element.9), channel_id=1, source_target_pairs={{8,0},{16,8},{24,16},{9,1},{17,9},{25,17},{10,2},{18,10},{26,18},{... | collective-permute-start | bytes 10616840 | tf_op jit(solution)/shard_map/ppermute | solution.py:27
  185.9 29.6 %copy-start.1 = (f32[4,1536,32]{1,2,0:T(8,128)S(1)}, f32[4,1536,32]{1,2,0:T(8,128)}, u32[]{:S(2)}) copy-start(f32[4,1536,32]{1,2,0:T(8,128)} %get-tuple-element.24) | copy-start | bytes 2359300
  185.9 29.6 %copy-start.2 = (f32[4,1536,32]{1,2,0:T(8,128)S(1)}, f32[4,1536,32]{1,2,0:T(8,128)}, u32[]{:S(2)}) copy-start(f32[4,1536,32]{1,2,0:T(8,128)} %get-tuple-element.25) | copy-start | bytes 2359300
  237.2 142.2 %all-to-all-start = ((f32[4,64,6144]{2,1,0:T(8,128)}), f32[4,64,6144]{2,1,0:T(8,128)}, u32[]{:S(2)}, u32[]{:S(2)}) async-start(f32[4,64,6144]{2,1,0:T(8,128)} %fusion.30), calls=%async_computation | async-start | bytes 12582912 | tf_op jit(solution)/shard_map/all_to_all | solution.py:237
  308.7 729.5 %reduce-scatter.5.cloned.1.call-start = ((), (), s32[]{:S(2)}) async-start(), calls=%async_computation.10 | async-start | bytes 4718592 | tf_op jit(solution)/shard_map/reduce_scatter | solution.py:253
  479.8 27.3 %copy-start.5 = (s32[4,1,32]{2,1,0:T(1,128)S(1)}, s32[4,1,32]{2,1,0:T(1,128)}, u32[]{:S(2)}) copy-start(s32[4,1,32]{2,1,0:T(1,128)} %get-tuple-element.14) | copy-start | bytes 1540
  501.7 76.1 %all-to-all-start.1 = ((f32[4,64,6144]{2,1,0:T(8,128)}), f32[4,64,6144]{2,1,0:T(8,128)}, u32[]{:S(2)}, u32[]{:S(2)}) async-start(f32[4,64,6144]{2,1,0:T(8,128)} %fusion.33), calls=%async_computation.2 | async-start | bytes 12582912 | tf_op jit(solution)/shard_map/all_to_all | solution.py:237
  507.0 531.2 %reduce-scatter.7.cloned.1.call-start = ((), (), s32[]{:S(2)}) async-start(), calls=%async_computation.11 | async-start | bytes 4718592 | tf_op jit(solution)/shard_map/reduce_scatter | solution.py:253
  667.3 27.3 %copy-start.4 = (s32[4,1,32]{2,1,0:T(1,128)S(1)}, s32[4,1,32]{2,1,0:T(1,128)}, u32[]{:S(2)}) copy-start(s32[4,1,32]{2,1,0:T(1,128)} %get-tuple-element.13) | copy-start | bytes 1540
  689.1 76.1 %all-to-all-start.2 = ((f32[4,64,6144]{2,1,0:T(8,128)}), f32[4,64,6144]{2,1,0:T(8,128)}, u32[]{:S(2)}, u32[]{:S(2)}) async-start(f32[4,64,6144]{2,1,0:T(8,128)} %fusion.36), calls=%async_computation.4 | async-start | bytes 12582912 | tf_op jit(solution)/shard_map/all_to_all | solution.py:237
  694.5 343.8 %reduce-scatter.9.cloned.1.call-start = ((), (), s32[]{:S(2)}) async-start(), calls=%async_computation.12 | async-start | bytes 4718592 | tf_op jit(solution)/shard_map/reduce_scatter | solution.py:253
  854.6 272.0 %reduce-scatter.11.cloned.1.call-start = ((), (), s32[]{:S(2)}) async-start(), calls=%async_computation.13 | async-start | bytes 4718592 | tf_op jit(solution)/shard_map/reduce_scatter | solution.py:253
Sparse Core Ops, SparseCore 0:
  85.2 85.4 all-gather.1
  479.9 88.3 reduce-scatter.4
  667.4 88.1 reduce-scatter.6
  854.7 88.1 reduce-scatter.8
  1038.3 88.2 reduce-scatter.10
